TPU v7x, 32 devices: a whole 2x2x4 slice. The times are simulated.
32 devices in a mesh: sample: 2 (over y), space: 8 (over z, x), node: 2 (over core).
Axes of the slice: x: 2, y: 2, z: 4, core: 2. Of those that a mesh axis runs over, the one named last changes fastest.
Arguments:
- initial: float32 [256, 24, 256], P(('sample', 'space')), parts along dimension 0, may hold values from -2.5 to 2.5
- diffusivity: float32 [256, 24, 256], P(('sample', 'space')), parts along dimension 0, may hold values from 0.05 to 0.5
- velocity: float32 [256, 24, 256], P(('sample', 'space')), parts along dimension 0, may hold values from -1 to 1
- growth_rate: float32 [256, 24, 256], P(('sample', 'space')), parts along dimension 0, may hold values from 0.25 to 2
- block_planes: int32 [8], replicated, may hold values from 1 to 16, 64 in all
Outputs:
- node_states: float32 [8, 256, 24, 256], P('node', ('sample', 'space')), parts along dimension 1
- node_rhs: float32 [8, 256, 24, 256], P('node', ('sample', 'space')), parts along dimension 1
There are 2 independent parts, one for each index of `sample`. A program takes and returns all parts, laid end to end along the dimension named above; an argument that names none is the same for every part. Nothing has to cross between parts.
Inputs may be any that keep to these rules, and one draw needn't show every extreme that they name: `block_planes`: block sizes of the 8 blocks sum to 64; the largest is exactly 16.
All inputs are finite; a program needn't handle non-finite values.
Results may differ from a plain program's by a relative error of at most 0.0001.
Values sent between devices are 32-bit elements; how exact they have to be, the bound alone decides.
A program may use at most 64 MiB of HBM per device.

v0:
```python
import math

import jax
import jax.numpy as jnp
from jax import lax
from jax.sharding import PartitionSpec as P

M = 8
SWEEPS = 2


step_length = 0.1


def with_halo(block, sides, width):
    for axis, dim in sides:
        count = lax.axis_size(axis)
        forward = [(i, i + 1) for i in range(count - 1)]
        backward = [(target, source) for source, target in forward]
        low = lax.ppermute(
            lax.slice_in_dim(block, block.shape[dim] - width, None, axis=dim), axis, forward
        )
        high = lax.ppermute(lax.slice_in_dim(block, 0, width, axis=dim), axis, backward)
        block = jnp.concatenate([low, block, high], axis=dim)
    return block


def legendre_values(order, position):
    previous_value = 1.0
    current_value = position
    for degree in range(2, order + 1):
        previous_value, current_value = (
            current_value,
            ((2 * degree - 1) * position * current_value - (degree - 1) * previous_value) / degree,
        )
    derivative = order * (position * current_value - previous_value) / (position * position - 1.0)
    return (current_value, derivative)


def collocation(count):
    descending = []
    for root_index in range(count):
        position = math.cos(math.pi * (root_index + 0.75) / (count + 0.5))
        for newton_step in range(60):
            poly_value, poly_slope = legendre_values(count, position)
            position = position - poly_value / poly_slope
        descending.append((position + 1.0) / 2.0)
    node_times = descending[::-1]
    quad_rows = []
    for row_index in range(count):
        quad_row = []
        for basis_index in range(count):
            coefficients = [1.0]
            for other_index in range(count):
                if other_index != basis_index:
                    denominator = node_times[basis_index] - node_times[other_index]
                    expanded = [0.0] * (len(coefficients) + 1)
                    for exponent, coefficient in enumerate(coefficients):
                        expanded[exponent + 1] += coefficient / denominator
                        expanded[exponent] -= coefficient * node_times[other_index] / denominator
                    coefficients = expanded
            integral = 0.0
            for exponent, coefficient in enumerate(coefficients):
                integral += coefficient * node_times[row_index] ** (exponent + 1) / (exponent + 1)
            quad_row.append(integral)
        quad_rows.append(quad_row)
    return (node_times, quad_rows)


def evaluate(states, prev_last, next_first, diffusivity, velocity, growth_rate, length_rows):
    index = lax.broadcasted_iota(jnp.int32, (1, states.shape[1], 1, 1), 1)
    shifted = jnp.concatenate([states[:, 1:], next_first[:, None]], axis=1)
    upper = jnp.where(index == length_rows - 1, next_first[:, None], shifted)
    lower = jnp.concatenate([prev_last[:, None], states[:, :-1]], axis=1)
    padded = jnp.pad(states, ((0, 0), (0, 0), (1, 1), (1, 1)))
    across = (
        padded[:, :, 2:, 1:-1]
        + padded[:, :, :-2, 1:-1]
        + padded[:, :, 1:-1, 2:]
        + padded[:, :, 1:-1, :-2]
    )
    laplace = upper + lower + across - 6.0 * states
    rhs = (
        diffusivity * laplace
        - 0.5 * velocity * (upper - lower)
        + growth_rate * states
        - states * states * states
    )
    return jnp.where(index < length_rows, rhs, 0.0)


def pack_rims(field, length):
    first_plane = field[:, 0]
    last_plane = lax.dynamic_index_in_dim(field, length - 1, axis=1, keepdims=False)
    return jnp.stack([first_plane, last_plane], axis=1)


def state_halo(field, length):
    return with_halo(pack_rims(field, length), (("space", 1),), 1)


def on_device(initial, diffusivity, velocity, growth_rate, block_planes):
    cap = initial.shape[0]
    length = block_planes[lax.axis_index("space")]
    per_device = M // lax.axis_size("node")
    first_node = lax.axis_index("node") * per_device
    node_times, quad_table = collocation(M)
    quad = jnp.asarray(quad_table, jnp.float32)
    times_all = jnp.asarray(node_times, jnp.float32)
    local_quad = lax.dynamic_slice_in_dim(quad, first_node, per_device, 0)
    local_times = lax.dynamic_slice_in_dim(times_all, first_node, per_device, 0)
    base = initial[None]
    start_ext = with_halo(pack_rims(base, length), (("space", 1),), 1)
    rhs = evaluate(
        base, start_ext[:, 0], start_ext[:, 3], diffusivity, velocity, growth_rate, length
    )
    time_scale = local_times[:, None, None, None]
    states = base
    for sweep_index in range(SWEEPS):
        extended = rhs
        if sweep_index == 0:
            combo = time_scale * extended
        else:
            flat = extended.reshape(extended.shape[0], -1)
            summed = jnp.dot(
                local_quad,
                lax.all_gather(flat, "node", axis=0, tiled=True),
                precision=lax.Precision.HIGHEST,
            )
            combo = summed.reshape(extended.shape)
        states = base + step_length * combo
        state_ext = state_halo(states, length)
        prev_last = state_ext[:, 0]
        next_first = state_ext[:, 3]
        rhs = evaluate(states, prev_last, next_first, diffusivity, velocity, growth_rate, length)
    index = lax.broadcasted_iota(jnp.int32, (1, cap, 1, 1), 1)
    states = jnp.where(index < length, states, 0.0)
    return (states, rhs)


def solution(mesh):
    placed = (
        P(("sample", "space"), None, None),
        P(("sample", "space"), None, None),
        P(("sample", "space"), None, None),
        P(("sample", "space"), None, None),
        P(),
    )
    return jax.shard_map(
        on_device,
        mesh=mesh,
        in_specs=placed,
        out_specs=(
            P("node", ("sample", "space"), None, None),
            P("node", ("sample", "space"), None, None),
        ),
        check_vma=False,
    )
```

profile of v0, /device:TPU:0, one launch (start us, length us, event | category | flops | bytes accessed | tf_op | source)
XLA Modules:
  0.0 76.3 jit_solution(17639033841099617634)
XLA Ops:
  7.3 0.8 %slice.84 = f32[1,1,24,256]{3,2,1,0:T(8,128)S(1)} slice(f32[1,16,24,256]{3,2,1,0:T(8,128)} %bitcast.39), slice={[0:1], [0:1], [0:24], [0:256]} | slice | bytes 49152 | tf_op jit(solution)/shard_map/slice | solution.py:93
  8.1 1.3 %collective-permute-start = (f32[1,1,24,256]{3,2,1,0:T(8,128)S(1)}, f32[1,1,24,256]{3,2,1,0:T(8,128)S(1)}, u32[]{:S(2)}, u32[]{:S(2)}) collective-permute-start(f32[1,1,24,256]{3,2,1,0:T(8,128)S(1)} %slice.84), channel_id=1, source_target_pairs={{2,0},{4,2},{6,4},{8,6},{10,8},{12,10},{14,12},{3,1},{5,3},{7,5},{... | collective-permute-start | bytes 73736 | tf_op jit(solution)/shard_map/ppermute | solution.py:23
  9.4 1.2 %dynamic_slice.20 = s32[1]{0:T(128)} dynamic-slice(s32[8]{0:T(128)} %param.11, s32[]{:T(128)S(6)} %select_n.49), dynamic_slice_sizes={1} | dynamic-slice | bytes 12 | tf_op jit(solution)/shard_map/dynamic_slice | solution.py:104
  11.9 0.7 dynamic-slice_bitcast_fusion
  12.7 5.5 %collective-permute-start.1 = (f32[1,1,24,256]{3,2,1,0:T(8,128)S(1)}, f32[1,1,24,256]{3,2,1,0:T(8,128)S(1)}, u32[]{:S(2)}, u32[]{:S(2)}) collective-permute-start(f32[1,1,24,256]{3,2,1,0:T(8,128)S(1)} %dynamic-slice_bitcast_fusion), channel_id=1, source_target_pairs={{0,2},{2,4},{4,6},{6,8},{8,10},{10,12},{12,14},{1,3},{3,5},{5,7},{... | collective-permute-start | bytes 73736 | tf_op jit(solution)/shard_map/ppermute | solution.py:20
  18.2 1.3 %slice_bitcast_fusion = (f32[15,24,256]{2,1,0:T(8,128)S(1)}, f32[15,24,256]{2,1,0:T(8,128)S(1)}, f32[1,15,24,256]{3,2,1,0:T(8,128)S(1)}, f32[1,15,24,256]{3,2,1,0:T(8,128)S(1)}) fusion(f32[1,16,24,256]{3,2,1,0:T(8,128)} %bitcast.40), kind=kLoop, calls=%fused_computation.69 | loop fusion | bytes 2211840 | tf_op jit(solution)/shard_map/concatenate | solution.py:74
  19.5 0.7 iota_compare_fusion
  20.3 0.6 fusion.23
  21.1 1.3 %collective-permute-start.2 = (f32[4,1,24,256]{3,2,1,0:T(8,128)S(1)}, f32[4,1,24,256]{3,2,1,0:T(8,128)S(1)}, u32[]{:S(2)}, u32[]{:S(2)}) collective-permute-start(f32[4,1,24,256]{3,2,1,0:T(8,128)S(1)} %get-tuple-element.10), channel_id=1, source_target_pairs={{2,0},{4,2},{6,4},{8,6},{10,8},{12,10},{14,12},{3,1},{5,3},{7,5},{... | collective-permute-start | bytes 294920 | tf_op jit(solution)/shard_map/ppermute | solution.py:23
  22.4 5.5 %collective-permute-start.3 = (f32[4,1,24,256]{3,2,1,0:T(8,128)S(1)}, f32[4,1,24,256]{3,2,1,0:T(8,128)S(1)}, u32[]{:S(2)}, u32[]{:S(2)}) collective-permute-start(f32[4,1,24,256]{3,2,1,0:T(8,128)S(1)} %get-tuple-element.11), channel_id=1, source_target_pairs={{0,2},{2,4},{4,6},{6,8},{8,10},{10,12},{12,14},{1,3},{3,5},{5,7},{... | collective-permute-start | bytes 294920 | tf_op jit(solution)/shard_map/ppermute | solution.py:20
  28.2 0.4 collective-permute-done.2
  28.5 1.9 %collective-permute-done.3 = f32[4,1,24,256]{3,2,1,0:T(8,128)S(1)} collective-permute-done((f32[4,1,24,256]{3,2,1,0:T(8,128)S(1)}, f32[4,1,24,256]{3,2,1,0:T(8,128)S(1)}, u32[]{:S(2)}, u32[]{:S(2)}) %collective-permute-start.3) | collective-permute-done | bytes 98336 | tf_op jit(solution)/shard_map/ppermute | solution.py:20
  30.4 1.9 %fusion.1 = f32[4,16,24,256]{3,2,1,0:T(8,128)S(1)} fusion(f32[4,16,24,256]{3,2,1,0:T(8,128)S(1)} %multiply_add_fusion, f32[4,15,24,256]{3,2,1,0:T(8,128)S(1)} %get-tuple-element.9, f32[4,1,24,256]{3,2,1,0:T(8,128)S(1)} %collective-permute-done.3, f32[4,1,24,256]{3,2,1,0:T(8,128)S(1)} %collective-permute-done.2, f32[4,15,24,256]{3,2,1,0:T(8,128)S(1)} %get-tuple-element.8, ...), kind=kLoop, calls=%fused_computation.12 | loop fusion | flops 7864320 | bytes 7569440 | tf_op jit(solution)/shard_map/jit(_where)/select_n | solution.py:89
  32.4 1.9 %reshape.95 = f32[1,4,98304]{2,1,0:T(4,128)} reshape(f32[4,16,24,256]{3,2,1,0:T(8,128)S(1)} %fusion.1) | data formatting | bytes 3145728
  34.3 15.6 %all-gather.3.cloned.1.call-done = f32[2,4,98304]{2,1,0:T(4,128)} async-done(((f32[1,4,98304]{2,1,0:T(4,128)}), f32[2,4,98304]{2,1,0:T(4,128)}) %all-gather.3.cloned.1.call-update) | async-done | bytes 3145744 | tf_op jit(solution)/shard_map/all_gather | solution.py:127
  50.0 3.0 %reshape.96 = f32[8,98304]{1,0:T(8,128)S(1)} reshape(f32[2,4,98304]{2,1,0:T(4,128)} %all-gather.3.cloned.1.call-done) | data formatting | bytes 6291456
  52.9 2.8 %convolution_multiply_fusion = f32[4,98304]{1,0:T(4,128)S(1)} fusion(f32[8,98304]{1,0:T(8,128)S(1)} %reshape.96, f32[8,8]{1,0:T(8,128)S(1)} %copy-done.8, s32[]{:T(128)S(6)} %select_n.50), kind=kOutput, calls=%fused_computation | convolution fusion | flops 38141952 | bytes 4720644 | tf_op jit(solution)/shard_map/dot_general | solution.py:125
  55.7 0.3 copy.9
  56.0 1.4 %broadcast_select_fusion = (f32[4,16,24,256]{3,2,1,0:T(8,128)}, f32[4,16,24,256]{3,2,1,0:T(8,128)S(1)}) fusion(pred[16]{0:T(512)(128)(4,1)S(1)} %get-tuple-element.17, f32[4,16,24,256]{3,2,1,0:T(8,128)S(1)} %bitcast.43, f32[16,24,256]{2,1,0:T(8,128)S(1)} %copy-done), kind=kLoop, calls=%fused_computation.40 | loop fusion | flops 786432 | bytes 5111824 | tf_op jit(solution)/shard_map/jit(_where)/select_n | solution.py:137
  57.4 1.3 %collective-permute-start.4 = (f32[4,1,24,256]{3,2,1,0:T(8,128)S(1)}, f32[4,1,24,256]{3,2,1,0:T(8,128)S(1)}, u32[]{:S(2)}, u32[]{:S(2)}) collective-permute-start(f32[4,1,24,256]{3,2,1,0:T(8,128)S(1)} %get-tuple-element.6), channel_id=1, source_target_pairs={{2,0},{4,2},{6,4},{8,6},{10,8},{12,10},{14,12},{3,1},{5,3},{7,5},{... | collective-permute-start | bytes 294920 | tf_op jit(solution)/shard_map/ppermute | solution.py:23
  58.8 4.7 %collective-permute-start.5 = (f32[4,1,24,256]{3,2,1,0:T(8,128)S(1)}, f32[4,1,24,256]{3,2,1,0:T(8,128)S(1)}, u32[]{:S(2)}, u32[]{:S(2)}) collective-permute-start(f32[4,1,24,256]{3,2,1,0:T(8,128)S(1)} %get-tuple-element.7), channel_id=1, source_target_pairs={{0,2},{2,4},{4,6},{6,8},{8,10},{10,12},{12,14},{1,3},{3,5},{5,7},{... | collective-permute-start | bytes 294920 | tf_op jit(solution)/shard_map/ppermute | solution.py:20
  63.7 0.6 collective-permute-done.4
  64.3 2.3 %collective-permute-done.5 = f32[4,1,24,256]{3,2,1,0:T(8,128)S(1)} collective-permute-done((f32[4,1,24,256]{3,2,1,0:T(8,128)S(1)}, f32[4,1,24,256]{3,2,1,0:T(8,128)S(1)}, u32[]{:S(2)}, u32[]{:S(2)}) %collective-permute-start.5) | collective-permute-done | bytes 98336 | tf_op jit(solution)/shard_map/ppermute | solution.py:20
  66.6 2.8 %fusion.3 = f32[4,16,24,256]{3,2,1,0:T(8,128)} fusion(f32[4,16,24,256]{3,2,1,0:T(8,128)S(1)} %get-tuple-element.3, f32[4,15,24,256]{3,2,1,0:T(8,128)S(1)} %get-tuple-element.5, f32[4,1,24,256]{3,2,1,0:T(8,128)S(1)} %collective-permute-done.5, f32[4,1,24,256]{3,2,1,0:T(8,128)S(1)} %collective-permute-done.4, f32[4,15,24,256]{3,2,1,0:T(8,128)S(1)} %get-tuple-element.4, ...), kind=kLoop, calls=%fused_computation.14 | loop fusion | flops 7864320 | bytes 7569440 | tf_op jit(solution)/shard_map/jit(_where)/select_n | solution.py:89
  (31 shorter events, 1.0 us)
Async XLA Ops:
  7.2 13.0 %copy-start.9 = (f32[8]{0:T(128)S(1)}, f32[8]{0:T(128)}, u32[]{:S(2)}) copy-start(f32[8]{0:T(128)} %constant.44.clone) | copy-start | bytes 100
  7.2 12.3 %copy-start.7 = (f32[16,24,256]{2,1,0:T(8,128)S(1)}, f32[16,24,256]{2,1,0:T(8,128)}, u32[]{:S(2)}) copy-start(f32[16,24,256]{2,1,0:T(8,128)} %param.9) | copy-start | bytes 1179652
  7.2 42.8 %all-gather.3.cloned.1.call-start = ((), (), s32[]{:S(2)}) async-start(), calls=%async_computation | async-start | bytes 4718592 | tf_op jit(solution)/shard_map/all_gather | solution.py:127
  7.2 13.1 %copy-start = (f32[16,24,256]{2,1,0:T(8,128)S(1)}, f32[16,24,256]{2,1,0:T(8,128)}, u32[]{:S(2)}) copy-start(f32[16,24,256]{2,1,0:T(8,128)} %param.7) | copy-start | bytes 1179652
  7.2 13.0 %copy-start.1 = (f32[16,24,256]{2,1,0:T(8,128)S(1)}, f32[16,24,256]{2,1,0:T(8,128)}, u32[]{:S(2)}) copy-start(f32[16,24,256]{2,1,0:T(8,128)} %param.8) | copy-start | bytes 1179652
  7.3 13.0 %copy-start.3 = (f32[16,24,256]{2,1,0:T(8,128)S(1)}, f32[16,24,256]{2,1,0:T(8,128)}, u32[]{:S(2)}) copy-start(f32[16,24,256]{2,1,0:T(8,128)} %param.10) | copy-start | bytes 1179652
  8.1 12.2 %collective-permute-start = (f32[1,1,24,256]{3,2,1,0:T(8,128)S(1)}, f32[1,1,24,256]{3,2,1,0:T(8,128)S(1)}, u32[]{:S(2)}, u32[]{:S(2)}) collective-permute-start(f32[1,1,24,256]{3,2,1,0:T(8,128)S(1)} %slice.84), channel_id=1, source_target_pairs={{2,0},{4,2},{6,4},{8,6},{10,8},{12,10},{14,12},{3,1},{5,3},{7,5},{... | collective-permute-start | bytes 73736 | tf_op jit(solution)/shard_map/ppermute | solution.py:23
  12.7 7.6 %collective-permute-start.1 = (f32[1,1,24,256]{3,2,1,0:T(8,128)S(1)}, f32[1,1,24,256]{3,2,1,0:T(8,128)S(1)}, u32[]{:S(2)}, u32[]{:S(2)}) collective-permute-start(f32[1,1,24,256]{3,2,1,0:T(8,128)S(1)} %dynamic-slice_bitcast_fusion), channel_id=1, source_target_pairs={{0,2},{2,4},{4,6},{6,8},{8,10},{10,12},{12,14},{1,3},{3,5},{5,7},{... | collective-permute-start | bytes 73736 | tf_op jit(solution)/shard_map/ppermute | solution.py:20
  19.5 11.0 %copy-start.5 = (f32[16,24,256]{2,1,0:T(8,128)}, f32[16,24,256]{2,1,0:T(8,128)S(1)}, u32[]{:S(2)}) copy-start(f32[16,24,256]{2,1,0:T(8,128)S(1)} %broadcast_multiply_fusion) | copy-start | bytes 1179652
  21.1 7.4 %collective-permute-start.2 = (f32[4,1,24,256]{3,2,1,0:T(8,128)S(1)}, f32[4,1,24,256]{3,2,1,0:T(8,128)S(1)}, u32[]{:S(2)}, u32[]{:S(2)}) collective-permute-start(f32[4,1,24,256]{3,2,1,0:T(8,128)S(1)} %get-tuple-element.10), channel_id=1, source_target_pairs={{2,0},{4,2},{6,4},{8,6},{10,8},{12,10},{14,12},{3,1},{5,3},{7,5},{... | collective-permute-start | bytes 294920 | tf_op jit(solution)/shard_map/ppermute | solution.py:23
  22.4 8.0 %collective-permute-start.3 = (f32[4,1,24,256]{3,2,1,0:T(8,128)S(1)}, f32[4,1,24,256]{3,2,1,0:T(8,128)S(1)}, u32[]{:S(2)}, u32[]{:S(2)}) collective-permute-start(f32[4,1,24,256]{3,2,1,0:T(8,128)S(1)} %get-tuple-element.11), channel_id=1, source_target_pairs={{0,2},{2,4},{4,6},{6,8},{8,10},{10,12},{12,14},{1,3},{3,5},{5,7},{... | collective-permute-start | bytes 294920 | tf_op jit(solution)/shard_map/ppermute | solution.py:20
  34.3 18.6 %copy-start.8 = (f32[8,8]{1,0:T(8,128)S(1)}, f32[8,8]{1,0:T(8,128)}, u32[]{:S(2)}) copy-start(f32[8,8]{1,0:T(8,128)} %constant.43.clone) | copy-start | bytes 772
  57.4 6.9 %collective-permute-start.4 = (f32[4,1,24,256]{3,2,1,0:T(8,128)S(1)}, f32[4,1,24,256]{3,2,1,0:T(8,128)S(1)}, u32[]{:S(2)}, u32[]{:S(2)}) collective-permute-start(f32[4,1,24,256]{3,2,1,0:T(8,128)S(1)} %get-tuple-element.6), channel_id=1, source_target_pairs={{2,0},{4,2},{6,4},{8,6},{10,8},{12,10},{14,12},{3,1},{5,3},{7,5},{... | collective-permute-start | bytes 294920 | tf_op jit(solution)/shard_map/ppermute | solution.py:23
  58.7 7.8 %copy-start.2 = (f32[16,24,256]{2,1,0:T(8,128)S(1)}, f32[16,24,256]{2,1,0:T(8,128)}, u32[]{:S(2)}) copy-start(f32[16,24,256]{2,1,0:T(8,128)} %param.8) | copy-start | bytes 1179652
  58.8 7.8 %copy-start.4 = (f32[16,24,256]{2,1,0:T(8,128)S(1)}, f32[16,24,256]{2,1,0:T(8,128)}, u32[]{:S(2)}) copy-start(f32[16,24,256]{2,1,0:T(8,128)} %param.10) | copy-start | bytes 1179652
  58.8 7.8 %copy-start.6 = (f32[16,24,256]{2,1,0:T(8,128)S(1)}, f32[16,24,256]{2,1,0:T(8,128)}, u32[]{:S(2)}) copy-start(f32[16,24,256]{2,1,0:T(8,128)} %copy-done.5) | copy-start | bytes 1179652
  58.8 7.8 %collective-permute-start.5 = (f32[4,1,24,256]{3,2,1,0:T(8,128)S(1)}, f32[4,1,24,256]{3,2,1,0:T(8,128)S(1)}, u32[]{:S(2)}, u32[]{:S(2)}) collective-permute-start(f32[4,1,24,256]{3,2,1,0:T(8,128)S(1)} %get-tuple-element.7), channel_id=1, source_target_pairs={{0,2},{2,4},{4,6},{6,8},{8,10},{10,12},{12,14},{1,3},{3,5},{5,7},{... | collective-permute-start | bytes 294920 | tf_op jit(solution)/shard_map/ppermute | solution.py:20
Sparse Core Ops, SparseCore 0:
  34.4 15.4 all-gather.2
where the time goes:
time: 77.3 us; the launch traced here: 76.3 us
  waiting for transfers between devices  20.8 us (27%)
  starting transfers between devices  19.5 us (25%)
  between operations  15.6 us (20%)
  local copies, waits for them, and re-layouts  9.97 us (13%)
  other arithmetic  7.65 us (10%)
  matrix products  2.76 us (4%)
    all_gather x1, waiting for transfers between devices, on_device(): lax.all_gather(flat, 'node', axis=0, tiled=True)  15.6 us
    ppermute x3, starting transfers between devices, with_halo(): lax.ppermute(lax.slice_in_dim(block, block.shape[dim] - width, None, axis...  15.6 us
    unnamed x23, local copies, waits for them, and re-layouts  5.26 us
    select_n x2, other arithmetic, evaluate(): return jnp.where(index < length_rows, rhs, 0.0)  4.75 us
    ppermute x3, waiting for transfers between devices, with_halo(): lax.ppermute(lax.slice_in_dim(block, block.shape[dim] - width, None, axis...  4.16 us
    ppermute x3, starting transfers between devices, with_halo(): lax.ppermute(lax.slice_in_dim(block, 0, width, axis=dim), axis, backward)  3.86 us
    dot_general x1, matrix products, on_device(): jnp.dot(local_quad, lax.all_gather(flat, 'node', axis=0, tiled=True), pre...  2.76 us
  transfers between devices with their start and end apart: 7, of which 5 were waited for; matrix products, arithmetic and copies ran while one was open for 6% of the time, Pallas kernels for 0%

commit v1 on v0

v1 whole, which is shorter than its diff:
```python
import functools
import math

import jax
import jax.numpy as jnp
from jax import lax
from jax.experimental import pallas as pl
from jax.experimental.pallas import tpu as pltpu
from jax.sharding import PartitionSpec as P

M = 8
step_length = 0.1


def legendre_values(order, position):
    previous_value = 1.0
    current_value = position
    for degree in range(2, order + 1):
        previous_value, current_value = (
            current_value,
            ((2 * degree - 1) * position * current_value - (degree - 1) * previous_value) / degree,
        )
    derivative = order * (position * current_value - previous_value) / (position * position - 1.0)
    return (current_value, derivative)


def collocation(count):
    descending = []
    for root_index in range(count):
        position = math.cos(math.pi * (root_index + 0.75) / (count + 0.5))
        for newton_step in range(60):
            poly_value, poly_slope = legendre_values(count, position)
            position = position - poly_value / poly_slope
        descending.append((position + 1.0) / 2.0)
    node_times = descending[::-1]
    quad_rows = []
    for row_index in range(count):
        quad_row = []
        for basis_index in range(count):
            coefficients = [1.0]
            for other_index in range(count):
                if other_index != basis_index:
                    denominator = node_times[basis_index] - node_times[other_index]
                    expanded = [0.0] * (len(coefficients) + 1)
                    for exponent, coefficient in enumerate(coefficients):
                        expanded[exponent + 1] += coefficient / denominator
                        expanded[exponent] -= coefficient * node_times[other_index] / denominator
                    coefficients = expanded
            integral = 0.0
            for exponent, coefficient in enumerate(coefficients):
                integral += coefficient * node_times[row_index] ** (exponent + 1) / (exponent + 1)
            quad_row.append(integral)
        quad_rows.append(quad_row)
    return (node_times, quad_rows)


def moments():
    _, quad = collocation(M)
    scale = [step_length * sum(row) for row in quad]
    rows = []
    for row in quad:
        power = [
            step_length * sum(q * s**k for q, s in zip(row, scale)) for k in range(4)
        ]
        rows.append((power[0], power[1], -3.0 * power[2], -power[3]))
    return rows


def across(u):
    rows, lanes = u.shape
    tile = [u[i : i + 8] for i in range(0, rows, 8)]
    row = lax.broadcasted_iota(jnp.int32, (8, lanes), 0)
    nil = jnp.zeros((8, lanes), u.dtype)
    down = [nil] + [pltpu.roll(t, 1, 0) for t in tile]
    rise = [pltpu.roll(t, 7, 0) for t in tile] + [nil]
    along_x = jnp.concatenate(
        [
            jnp.where(row == 0, down[k], down[k + 1]) + jnp.where(row == 7, rise[k + 1], rise[k])
            for k in range(len(tile))
        ],
        axis=0,
    )
    half = [u[:, i : i + 128] for i in range(0, lanes, 128)]
    lane = lax.broadcasted_iota(jnp.int32, (rows, 128), 1)
    nil = jnp.zeros((rows, 128), u.dtype)
    down = [nil] + [pltpu.roll(t, 1, 1) for t in half]
    rise = [pltpu.roll(t, 127, 1) for t in half] + [nil]
    along_y = jnp.concatenate(
        [
            jnp.where(lane == 0, down[k], down[k + 1])
            + jnp.where(lane == 127, rise[k + 1], rise[k])
            for k in range(len(half))
        ],
        axis=1,
    )
    return along_x + along_y


def factors(d_ref, v_ref, g_ref, p):
    d = d_ref[p]
    v = 0.5 * v_ref[p]
    return d, d - v, d + v, g_ref[p] - 6.0 * d


def exchange_kernel(
    bp, u_hbm, d_hbm, v_hbm, g_hbm, r_ref, a_ref, halo_ref,
    u_ref, d_ref, v_ref, g_ref, out, got, load_sem, send_sem, recv_sem,
):
    me = lax.axis_index("space")
    count = lax.axis_size("space")
    has_left = me > 0
    has_right = me < count - 1
    cap = u_ref.shape[0]
    loads = [
        pltpu.make_async_copy(src, dst, load_sem.at[i])
        for i, (src, dst) in enumerate(
            [(u_hbm, u_ref), (d_hbm, d_ref), (v_hbm, v_ref), (g_hbm, g_ref)]
        )
    ]
    for load in loads:
        load.start()
    barrier = pltpu.get_barrier_semaphore()

    @pl.when(has_left)
    def _():
        pl.semaphore_signal(
            barrier, inc=1, device_id={"space": me - 1}, device_id_type=pl.DeviceIdType.MESH
        )

    @pl.when(has_right)
    def _():
        pl.semaphore_signal(
            barrier, inc=1, device_id={"space": me + 1}, device_id_type=pl.DeviceIdType.MESH
        )

    last = jnp.clip(bp[me] - 1, 0, cap - 1)
    nil = jnp.zeros(u_ref.shape[1:], jnp.float32)

    @pl.when(jnp.logical_not(has_left))
    def _():
        for k in range(3):
            got[k, 0] = nil

    @pl.when(jnp.logical_not(has_right))
    def _():
        for k in range(3):
            got[k, 1] = nil

    def copy(k, side):
        return pltpu.make_async_remote_copy(
            src_ref=out.at[k, side],
            dst_ref=got.at[k, side],
            send_sem=send_sem.at[k, side],
            recv_sem=recv_sem.at[k, side],
            device_id={"space": me + 1 if side == 0 else me - 1},
            device_id_type=pl.DeviceIdType.MESH,
        )

    def send(k):
        @pl.when(has_right)
        def _():
            copy(k, 0).start()

        @pl.when(has_left)
        def _():
            copy(k, 1).start()

    def receive(k):
        @pl.when(has_left)
        def _():
            copy(k, 0).wait_recv()

        @pl.when(has_right)
        def _():
            copy(k, 1).wait_recv()

    def beside(ref, p, k):
        low = jnp.where(p == 0, got[k, 0], ref[jnp.maximum(p - 1, 0)])
        high = jnp.where(p == last, got[k, 1], ref[jnp.minimum(p + 1, cap - 1)])
        return low, high

    def first_rhs(p):
        d, rise, fall, own = factors(d_ref, v_ref, g_ref, p)
        low, high = beside(u_ref, p, 0)
        u = u_ref[p]
        return d * across(u) + rise * high + fall * low + (own - u * u) * u

    def slope(p):
        d, rise, fall, own = factors(d_ref, v_ref, g_ref, p)
        low, high = beside(r_ref, p, 1)
        u = u_ref[p]
        r = r_ref[p]
        return d * across(r) + rise * high + fall * low + (own - 3.0 * (u * u)) * r

    loads[0].wait()
    out[0, 0] = u_ref[last]
    out[0, 1] = u_ref[0]

    pl.semaphore_wait(barrier, has_left.astype(jnp.int32) + has_right.astype(jnp.int32))
    send(0)
    for load in loads[1:]:
        load.wait()
    receive(0)
    out[1, 0] = first_rhs(last)
    out[1, 1] = first_rhs(0)
    send(1)

    def fill_r(p, carry):
        r_ref[p] = first_rhs(p)
        return carry

    lax.fori_loop(0, cap, fill_r, 0)
    receive(1)
    out[2, 0] = slope(last)
    out[2, 1] = slope(0)
    send(2)

    def fill_a(p, carry):
        a_ref[p] = slope(p)
        return carry

    lax.fori_loop(0, cap, fill_a, 0)
    receive(2)
    for k in range(3):
        for side in range(2):
            halo_ref[k, side] = got[k, side]
    for k in range(3):
        @pl.when(has_right)
        def _(k=k):
            copy(k, 0).wait_send()

        @pl.when(has_left)
        def _(k=k):
            copy(k, 1).wait_send()


def finish_kernel(
    table, chunk, bp, u_ref, d_ref, v_ref, g_ref, r_ref, a_ref, halo_ref, s_hbm, f_hbm,
    s_ref, f_ref, sem,
):
    nodes = s_ref.shape[0]
    cap = u_ref.shape[0]
    length = bp[lax.axis_index("space")]
    last = jnp.clip(length - 1, 0, cap - 1)
    node = lax.axis_index("node")
    weights = []
    for m in range(nodes):
        picked = [jnp.float32(x) for x in table[m]]
        for n in range(1, M // nodes):
            picked = [
                jnp.where(node == n, jnp.float32(x), y)
                for x, y in zip(table[n * nodes + m], picked)
            ]
        weights.append(picked)

    def states_of(u, r, a):
        rr = r * r
        ur = u * rr
        cube = rr * r
        return [u + w[0] * r + w[1] * a + (w[2] * ur + w[3] * cube) for w in weights]

    for side in range(2):
        values = states_of(halo_ref[0, side], halo_ref[1, side], halo_ref[2, side])
        for m in range(nodes):
            s_ref[m, side * (cap + 1)] = values[m]

    copies = []

    def put(src, dst, lo, which):
        c = pltpu.make_async_copy(
            src, dst.at[:, pl.ds(lo, chunk)], sem.at[which, lo // chunk]
        )
        c.start()
        copies.append(c)

    for lo in range(0, cap, chunk):

        def fill_s(p, carry):
            values = states_of(u_ref[p], r_ref[p], a_ref[p])
            live = p < length
            for m in range(nodes):
                s_ref[m, p + 1] = jnp.where(live, values[m], 0.0)
            return carry

        lax.fori_loop(lo, lo + chunk, fill_s, 0)
        put(s_ref.at[:, pl.ds(lo + 1, chunk)], s_hbm, lo, 0)
    for lo in range(0, cap, chunk):

        def fill_f(p, carry):
            d, rise, fall, own = factors(d_ref, v_ref, g_ref, p)
            live = p < length
            after = jnp.where(p == last, cap + 1, p + 2)
            for m in range(nodes):
                s = s_ref[m, p + 1]
                f = (
                    d * across(s)
                    + rise * s_ref[m, after]
                    + fall * s_ref[m, p]
                    + (own - s * s) * s
                )
                f_ref[m, p] = jnp.where(live, f, 0.0)
            return carry

        lax.fori_loop(lo, lo + chunk, fill_f, 0)
        put(f_ref.at[:, pl.ds(lo, chunk)], f_hbm, lo, 1)
    for c in copies:
        c.wait()


def on_device(initial, diffusivity, velocity, growth_rate, block_planes):
    shape = initial.shape
    plane = shape[1:]
    nodes = M // lax.axis_size("node")
    chunk = 4
    fields = (initial, diffusivity, velocity, growth_rate)
    vmem = pl.BlockSpec(memory_space=pltpu.VMEM)
    smem = pl.BlockSpec(memory_space=pltpu.SMEM)
    anyspace = pl.BlockSpec(memory_space=pl.ANY)
    field = jax.ShapeDtypeStruct(shape, jnp.float32)
    r, a, halo = pl.pallas_call(
        exchange_kernel,
        out_shape=(field, field, jax.ShapeDtypeStruct((3, 2) + plane, jnp.float32)),
        in_specs=[smem] + [anyspace] * 4,
        out_specs=(vmem,) * 3,
        scratch_shapes=[pltpu.VMEM(shape, jnp.float32)] * 4
        + [
            pltpu.VMEM((3, 2) + plane, jnp.float32),
            pltpu.VMEM((3, 2) + plane, jnp.float32),
            pltpu.SemaphoreType.DMA((4,)),
            pltpu.SemaphoreType.DMA((3, 2)),
            pltpu.SemaphoreType.DMA((3, 2)),
        ],
        compiler_params=pltpu.CompilerParams(
            collective_id=0, has_side_effects=True, vmem_limit_bytes=24 << 20
        ),
        name="exchange",
    )(block_planes, *fields)
    whole = jax.ShapeDtypeStruct((nodes,) + shape, jnp.float32)
    states, rhs = pl.pallas_call(
        functools.partial(finish_kernel, moments(), chunk),
        out_shape=(whole, whole),
        in_specs=[smem] + [vmem] * 7,
        out_specs=(anyspace,) * 2,
        scratch_shapes=[
            pltpu.VMEM((nodes, shape[0] + 2) + plane, jnp.float32),
            pltpu.VMEM((nodes,) + shape, jnp.float32),
            pltpu.SemaphoreType.DMA((2, shape[0] // chunk)),
        ],
        compiler_params=pltpu.CompilerParams(vmem_limit_bytes=24 << 20),
        name="finish",
    )(block_planes, *fields, r, a, halo)
    return (states, rhs)


def solution(mesh):
    placed = (
        P(("sample", "space"), None, None),
        P(("sample", "space"), None, None),
        P(("sample", "space"), None, None),
        P(("sample", "space"), None, None),
        P(),
    )
    return jax.shard_map(
        on_device,
        mesh=mesh,
        in_specs=placed,
        out_specs=(
            P("node", ("sample", "space"), None, None),
            P("node", ("sample", "space"), None, None),
        ),
        check_vma=False,
    )
```

time: 77.3 us -> 24.4 us (0.32)
  waiting for transfers between devices: 20.8 us -> 0 us
  starting transfers between devices: 19.5 us -> 0 us
  Pallas kernels: 0 us -> 18.8 us
  between operations: 15.6 us -> 0.65 us
  other arithmetic: 7.65 us -> 0 us
  local copies, waits for them, and re-layouts: 9.97 us -> 4.63 us
  matrix products: 2.76 us -> 0 us
    ppermute x6 -> x0, starting transfers between devices: 19.5 us -> none  [the longest x3 15.6 us: with_halo(): lax.ppermute(lax.slice_in_dim(block, block.shape[dim] - width, None, axis...]
    pallas_call x0 -> x2, Pallas kernels: none -> 18.8 us  [the longest x1 14.8 us: on_device(): pl.pallas_call(exchange_kernel, out_shape=(field, field, jax.ShapeDtypeSt...]
    all_gather x1 -> x0, waiting for transfers between devices: 15.6 us -> none  [on_device(): lax.all_gather(flat, 'node', axis=0, tiled=True)]
    select_n x3 -> x0, other arithmetic: 6.16 us -> none  [the longest x2 4.75 us: evaluate(): return jnp.where(index < length_rows, rhs, 0.0)]
    ppermute x6 -> x0, waiting for transfers between devices: 5.16 us -> none  [the longest x3 4.16 us: with_halo(): lax.ppermute(lax.slice_in_dim(block, block.shape[dim] - width, None, axis...]
    dot_general x1 -> x0, matrix products: 2.76 us -> none  [on_device(): jnp.dot(local_quad, lax.all_gather(flat, 'node', axis=0, tiled=True), pre...]
    dynamic_slice x3 -> x0, local copies, waits for them, and re-layouts: 2.06 us -> none  [the longest x1 1.24 us: on_device(): length = block_planes[lax.axis_index('space')]]
    slice x5 -> x0, local copies, waits for them, and re-layouts: 1.37 us -> none  [the longest x3 0.88 us: pack_rims(): first_plane = field[:, 0]]
  transfers between devices with their start and end apart: 7 -> 0, of which waited for: 5 -> 0; matrix products, arithmetic and copies ran while one was open for 6% -> 0% of each run, Pallas kernels for 0% -> 0%
where the time goes in v1:
time: 24.4 us; the launch traced here: 24.1 us
  Pallas kernels  18.8 us (77%)
  local copies, waits for them, and re-layouts  4.63 us (19%)
  between operations  0.65 us (3%)
    pallas_call x1, Pallas kernels, on_device(): pl.pallas_call(exchange_kernel, out_shape=(field, field, jax.ShapeDtypeSt...  14.8 us
    unnamed x10, local copies, waits for them, and re-layouts  4.63 us
    pallas_call x1, Pallas kernels, on_device(): pl.pallas_call(functools.partial(finish_kernel, moments(), chunk), out_sh...  4.08 us

profile of v1, /device:TPU:0, one launch (start us, length us, event | category | flops | bytes accessed | tf_op | source)
XLA Modules:
  0.0 24.1 jit_solution(7688295195548821338)
XLA Ops:
  0.6 0.0 copy-start
  0.6 1.0 %copy-done = f32[16,24,256]{2,1,0:T(8,128)S(1)} copy-done((f32[16,24,256]{2,1,0:T(8,128)S(1)}, f32[16,24,256]{2,1,0:T(8,128)}, u32[]{:S(2)}) %copy-start) | copy-done | bytes 393240
  1.6 0.0 copy-start.1
  1.6 1.0 %copy-done.1 = f32[16,24,256]{2,1,0:T(8,128)S(1)} copy-done((f32[16,24,256]{2,1,0:T(8,128)S(1)}, f32[16,24,256]{2,1,0:T(8,128)}, u32[]{:S(2)}) %copy-start.1) | copy-done | bytes 393240
  2.6 0.0 copy-start.2
  2.6 1.0 %copy-done.2 = f32[16,24,256]{2,1,0:T(8,128)S(1)} copy-done((f32[16,24,256]{2,1,0:T(8,128)S(1)}, f32[16,24,256]{2,1,0:T(8,128)}, u32[]{:S(2)}) %copy-start.2) | copy-done | bytes 393240
  3.6 0.0 copy-start.3
  3.6 1.0 %copy-done.3 = f32[16,24,256]{2,1,0:T(8,128)S(1)} copy-done((f32[16,24,256]{2,1,0:T(8,128)S(1)}, f32[16,24,256]{2,1,0:T(8,128)}, u32[]{:S(2)}) %copy-start.3) | copy-done | bytes 393240
  4.6 0.0 copy-start.4
  4.6 0.7 %copy-done.4 = s32[8]{0:T(128)S(1)} copy-done((s32[8]{0:T(128)S(1)}, s32[8]{0:T(128)}, u32[]{:S(2)}) %copy-start.4) | copy-done | bytes 56
  5.3 14.8 %exchange.1 = (f32[16,24,256]{2,1,0:T(8,128)S(1)}, f32[16,24,256]{2,1,0:T(8,128)S(1)}, f32[3,2,24,256]{3,2,1,0:T(8,128)S(1)}) custom-call(s32[8]{0:T(128)S(1)} %copy-done.4, f32[16,24,256]{2,1,0:T(8,128)S(1)} %copy-done, f32[16,24,256]{2,1,0:T(8,128)S(1)} %copy-done.1, f32[16,24,256]{2,1,0:T(8,128)S(1)} %copy-done.2, f32[16,24,256]{2,1,0:T(8,128)S(1)} %copy-done.3), custom_call_target="tpu_custom_call" | custom-call | tf_op jit(solution)/shard_map/exchange/pallas_call | solution.py:320
  20.0 4.1 %finish.1 = (f32[4,16,24,256]{3,2,1,0:T(8,128)}, f32[4,16,24,256]{3,2,1,0:T(8,128)}) custom-call(s32[8]{0:T(128)S(1)} %copy-done.4, f32[16,24,256]{2,1,0:T(8,128)S(1)} %copy-done, f32[16,24,256]{2,1,0:T(8,128)S(1)} %copy-done.1, f32[16,24,256]{2,1,0:T(8,128)S(1)} %copy-done.2, f32[16,24,256]{2,1,0:T(8,128)S(1)} %copy-done.3, ...), custom_call_target="tpu_custom_call" | custom-call | tf_op jit(solution)/shard_map/finish/pallas_call | solution.py:339
Async XLA Ops:
  0.6 1.0 %copy-start = (f32[16,24,256]{2,1,0:T(8,128)S(1)}, f32[16,24,256]{2,1,0:T(8,128)}, u32[]{:S(2)}) copy-start(f32[16,24,256]{2,1,0:T(8,128)} %u_ref.1) | copy-start | bytes 1179652
  1.6 1.0 %copy-start.1 = (f32[16,24,256]{2,1,0:T(8,128)S(1)}, f32[16,24,256]{2,1,0:T(8,128)}, u32[]{:S(2)}) copy-start(f32[16,24,256]{2,1,0:T(8,128)} %d_ref.1) | copy-start | bytes 1179652
  2.6 1.0 %copy-start.2 = (f32[16,24,256]{2,1,0:T(8,128)S(1)}, f32[16,24,256]{2,1,0:T(8,128)}, u32[]{:S(2)}) copy-start(f32[16,24,256]{2,1,0:T(8,128)} %v_ref.1) | copy-start | bytes 1179652
  3.6 1.0 %copy-start.3 = (f32[16,24,256]{2,1,0:T(8,128)S(1)}, f32[16,24,256]{2,1,0:T(8,128)}, u32[]{:S(2)}) copy-start(f32[16,24,256]{2,1,0:T(8,128)} %g_ref.1) | copy-start | bytes 1179652
  4.6 0.7 %copy-start.4 = (s32[8]{0:T(128)S(1)}, s32[8]{0:T(128)}, u32[]{:S(2)}) copy-start(s32[8]{0:T(128)} %bp.3) | copy-start | bytes 100

commit v2 on v1

v2 whole, which is shorter than its diff:
```python
import functools
import math

import jax
import jax.numpy as jnp
from jax import lax
from jax.experimental import pallas as pl
from jax.experimental.pallas import tpu as pltpu
from jax.sharding import PartitionSpec as P

M = 8
step_length = 0.1


def legendre_values(order, position):
    previous_value = 1.0
    current_value = position
    for degree in range(2, order + 1):
        previous_value, current_value = (
            current_value,
            ((2 * degree - 1) * position * current_value - (degree - 1) * previous_value) / degree,
        )
    derivative = order * (position * current_value - previous_value) / (position * position - 1.0)
    return (current_value, derivative)


def collocation(count):
    descending = []
    for root_index in range(count):
        position = math.cos(math.pi * (root_index + 0.75) / (count + 0.5))
        for newton_step in range(60):
            poly_value, poly_slope = legendre_values(count, position)
            position = position - poly_value / poly_slope
        descending.append((position + 1.0) / 2.0)
    node_times = descending[::-1]
    quad_rows = []
    for row_index in range(count):
        quad_row = []
        for basis_index in range(count):
            coefficients = [1.0]
            for other_index in range(count):
                if other_index != basis_index:
                    denominator = node_times[basis_index] - node_times[other_index]
                    expanded = [0.0] * (len(coefficients) + 1)
                    for exponent, coefficient in enumerate(coefficients):
                        expanded[exponent + 1] += coefficient / denominator
                        expanded[exponent] -= coefficient * node_times[other_index] / denominator
                    coefficients = expanded
            integral = 0.0
            for exponent, coefficient in enumerate(coefficients):
                integral += coefficient * node_times[row_index] ** (exponent + 1) / (exponent + 1)
            quad_row.append(integral)
        quad_rows.append(quad_row)
    return (node_times, quad_rows)


def moments():
    _, quad = collocation(M)
    scale = [step_length * sum(row) for row in quad]
    rows = []
    for row in quad:
        power = [
            step_length * sum(q * s**k for q, s in zip(row, scale)) for k in range(4)
        ]
        rows.append((power[0], power[1], -3.0 * power[2], -power[3]))
    return rows


def across(u):
    rows, lanes = u.shape
    tile = [u[i : i + 8] for i in range(0, rows, 8)]
    row = lax.broadcasted_iota(jnp.int32, (8, lanes), 0)
    nil = jnp.zeros((8, lanes), u.dtype)
    down = [nil] + [pltpu.roll(t, 1, 0) for t in tile]
    rise = [pltpu.roll(t, 7, 0) for t in tile] + [nil]
    along_x = jnp.concatenate(
        [
            jnp.where(row == 0, down[k], down[k + 1]) + jnp.where(row == 7, rise[k + 1], rise[k])
            for k in range(len(tile))
        ],
        axis=0,
    )
    half = [u[:, i : i + 128] for i in range(0, lanes, 128)]
    lane = lax.broadcasted_iota(jnp.int32, (rows, 128), 1)
    nil = jnp.zeros((rows, 128), u.dtype)
    down = [nil] + [pltpu.roll(t, 1, 1) for t in half]
    rise = [pltpu.roll(t, 127, 1) for t in half] + [nil]
    along_y = jnp.concatenate(
        [
            jnp.where(lane == 0, down[k], down[k + 1])
            + jnp.where(lane == 127, rise[k + 1], rise[k])
            for k in range(len(half))
        ],
        axis=1,
    )
    return along_x + along_y


def factors(d_ref, v_ref, g_ref, p):
    d = d_ref[p]
    v = 0.5 * v_ref[p]
    return d, d - v, d + v, g_ref[p] - 6.0 * d


def window_kernel(
    table,
    bp_hbm, u_hbm, d_hbm, v_hbm, g_hbm, s_ref, f_ref,
    bp, u_ref, d_ref, v_ref, g_ref, r_ref, a_ref, out, got, edge, load_sem, send_sem, recv_sem,
):
    me = lax.axis_index("space")
    count = lax.axis_size("space")
    has_left = me > 0
    has_right = me < count - 1
    cap = u_ref.shape[0]
    nodes = s_ref.shape[0]
    loads = [
        pltpu.make_async_copy(src, dst, load_sem.at[i])
        for i, (src, dst) in enumerate(
            [(bp_hbm, bp), (u_hbm, u_ref), (d_hbm, d_ref), (v_hbm, v_ref), (g_hbm, g_ref)]
        )
    ]
    for load in loads:
        load.start()
    barrier = pltpu.get_barrier_semaphore()

    @pl.when(has_left)
    def _():
        pl.semaphore_signal(
            barrier, inc=1, device_id={"space": me - 1}, device_id_type=pl.DeviceIdType.MESH
        )

    @pl.when(has_right)
    def _():
        pl.semaphore_signal(
            barrier, inc=1, device_id={"space": me + 1}, device_id_type=pl.DeviceIdType.MESH
        )

    nil = jnp.zeros(u_ref.shape[1:], jnp.float32)

    @pl.when(jnp.logical_not(has_left))
    def _():
        for k in range(3):
            got[k, 0] = nil

    @pl.when(jnp.logical_not(has_right))
    def _():
        for k in range(3):
            got[k, 1] = nil

    node = lax.axis_index("node")
    weights = []
    for m in range(nodes):
        picked = [jnp.float32(x) for x in table[m]]
        for n in range(1, M // nodes):
            picked = [
                jnp.where(node == n, jnp.float32(x), y)
                for x, y in zip(table[n * nodes + m], picked)
            ]
        weights.append(picked)

    def copy(k, side):
        return pltpu.make_async_remote_copy(
            src_ref=out.at[k, side],
            dst_ref=got.at[k, side],
            send_sem=send_sem.at[k, side],
            recv_sem=recv_sem.at[k, side],
            device_id={"space": me + 1 if side == 0 else me - 1},
            device_id_type=pl.DeviceIdType.MESH,
        )

    def send(k):
        @pl.when(has_right)
        def _():
            copy(k, 0).start()

        @pl.when(has_left)
        def _():
            copy(k, 1).start()

    def receive(k):
        @pl.when(has_left)
        def _():
            copy(k, 0).wait_recv()

        @pl.when(has_right)
        def _():
            copy(k, 1).wait_recv()

    loads[0].wait()
    length = bp[me]
    last = jnp.clip(length - 1, 0, cap - 1)

    def beside(ref, p, k):
        low = jnp.where(p == 0, got[k, 0], ref[jnp.maximum(p - 1, 0)])
        high = jnp.where(p == last, got[k, 1], ref[jnp.minimum(p + 1, cap - 1)])
        return low, high

    def first_rhs(p):
        d, rise, fall, own = factors(d_ref, v_ref, g_ref, p)
        low, high = beside(u_ref, p, 0)
        u = u_ref[p]
        return d * across(u) + rise * high + fall * low + (own - u * u) * u

    def slope(p):
        d, rise, fall, own = factors(d_ref, v_ref, g_ref, p)
        low, high = beside(r_ref, p, 1)
        u = u_ref[p]
        r = r_ref[p]
        return d * across(r) + rise * high + fall * low + (own - 3.0 * (u * u)) * r

    def states_of(u, r, a):
        rr = r * r
        ur = u * rr
        cube = rr * r
        return [u + w[0] * r + w[1] * a + (w[2] * ur + w[3] * cube) for w in weights]

    loads[1].wait()
    out[0, 0] = u_ref[last]
    out[0, 1] = u_ref[0]
    pl.semaphore_wait(barrier, has_left.astype(jnp.int32) + has_right.astype(jnp.int32))
    send(0)
    for load in loads[2:]:
        load.wait()
    receive(0)
    out[1, 0] = first_rhs(last)
    out[1, 1] = first_rhs(0)
    send(1)

    def fill_r(p, carry):
        r_ref[p] = first_rhs(p)
        return carry

    lax.fori_loop(0, cap, fill_r, 0)
    receive(1)
    out[2, 0] = slope(last)
    out[2, 1] = slope(0)
    send(2)

    def fill_s(p, carry):
        values = states_of(u_ref[p], r_ref[p], slope(p))
        live = p < length
        for m in range(nodes):
            s_ref[m, p] = jnp.where(live, values[m], 0.0)
        return carry

    lax.fori_loop(0, cap, fill_s, 0)

    def fill_f(p, carry):
        d, rise, fall, own = factors(d_ref, v_ref, g_ref, p)
        live = p < length
        down = jnp.maximum(p - 1, 0)
        up = jnp.minimum(p + 1, cap - 1)
        fall = jnp.where(p == 0, 0.0, fall)
        rise = jnp.where(p == cap - 1, 0.0, rise)
        for m in range(nodes):
            s = s_ref[m, p]
            f = d * across(s) + rise * s_ref[m, up] + fall * s_ref[m, down] + (own - s * s) * s
            f_ref[m, p] = jnp.where(live, f, 0.0)
        return carry

    lax.fori_loop(0, cap, fill_f, 0)
    receive(2)
    _, _, fall, _ = factors(d_ref, v_ref, g_ref, 0)
    values = states_of(got[0, 0], got[1, 0], got[2, 0])
    for m in range(nodes):
        f_ref[m, 0] += fall * values[m]
    _, rise, _, _ = factors(d_ref, v_ref, g_ref, last)
    values = states_of(got[0, 1], got[1, 1], got[2, 1])
    for m in range(nodes):
        edge[m] = rise * values[m]

    def fix(p, carry):
        for m in range(nodes):
            f_ref[m, p] += jnp.where(p == last, edge[m], 0.0)
        return carry

    lax.fori_loop(0, cap, fix, 0)
    for k in range(3):
        @pl.when(has_right)
        def _(k=k):
            copy(k, 0).wait_send()

        @pl.when(has_left)
        def _(k=k):
            copy(k, 1).wait_send()


def write_kernel(chunk, s_ref, f_ref, s_hbm, f_hbm, sem):
    copies = []
    for lo in range(0, s_ref.shape[1], chunk):
        part = pl.ds(lo, chunk)
        for i, (src, dst) in enumerate([(s_ref, s_hbm), (f_ref, f_hbm)]):
            copies.append(
                pltpu.make_async_copy(src.at[:, part], dst.at[:, part], sem.at[i, lo // chunk])
            )
    for c in copies:
        c.start()
    for c in copies:
        c.wait()


def on_device(initial, diffusivity, velocity, growth_rate, block_planes):
    shape = initial.shape
    plane = shape[1:]
    nodes = M // lax.axis_size("node")
    chunk = 4
    operands = [
        pltpu.with_memory_space_constraint(x, pltpu.HBM)
        for x in (block_planes, initial, diffusivity, velocity, growth_rate)
    ]
    vmem = pl.BlockSpec(memory_space=pltpu.VMEM)
    hbm = pl.BlockSpec(memory_space=pltpu.HBM)
    whole = jax.ShapeDtypeStruct((nodes,) + shape, jnp.float32)
    held = pl.pallas_call(
        functools.partial(window_kernel, moments()),
        out_shape=(whole, whole),
        in_specs=[hbm] * 5,
        out_specs=(vmem, vmem),
        scratch_shapes=[pltpu.SMEM(block_planes.shape, jnp.int32)]
        + [pltpu.VMEM(shape, jnp.float32)] * 6
        + [
            pltpu.VMEM((3, 2) + plane, jnp.float32),
            pltpu.VMEM((3, 2) + plane, jnp.float32),
            pltpu.VMEM((nodes,) + plane, jnp.float32),
            pltpu.SemaphoreType.DMA((5,)),
            pltpu.SemaphoreType.DMA((3, 2)),
            pltpu.SemaphoreType.DMA((3, 2)),
        ],
        compiler_params=pltpu.CompilerParams(
            collective_id=0, has_side_effects=True, vmem_limit_bytes=24 << 20
        ),
        name="window",
    )(*operands)
    return pl.pallas_call(
        functools.partial(write_kernel, chunk),
        out_shape=(whole, whole),
        in_specs=[vmem] * 2,
        out_specs=(hbm, hbm),
        scratch_shapes=[pltpu.SemaphoreType.DMA((2, shape[0] // chunk))],
        compiler_params=pltpu.CompilerParams(vmem_limit_bytes=24 << 20),
        name="write",
    )(*held)


def solution(mesh):
    placed = (
        P(("sample", "space"), None, None),
        P(("sample", "space"), None, None),
        P(("sample", "space"), None, None),
        P(("sample", "space"), None, None),
        P(),
    )
    return jax.shard_map(
        on_device,
        mesh=mesh,
        in_specs=placed,
        out_specs=(
            P("node", ("sample", "space"), None, None),
            P("node", ("sample", "space"), None, None),
        ),
        check_vma=False,
    )
```

time: 24.4 us -> 16.5 us (0.68)
  local copies, waits for them, and re-layouts: 4.63 us -> 0 us
  Pallas kernels: 18.8 us -> 15.7 us
    unnamed x10 -> x0, local copies, waits for them, and re-layouts: 4.63 us -> none
    pallas_call x2, Pallas kernels: 18.8 us -> 15.7 us  [the longest x1 13.9 us: on_device(): pl.pallas_call(functools.partial(window_kernel, moments()), out_shape=(wh...]
where the time goes in v2:
time: 16.5 us; the launch traced here: 16.3 us
  Pallas kernels  15.7 us (95%)
  between operations  0.64 us (4%)
    pallas_call x1, Pallas kernels, on_device(): pl.pallas_call(functools.partial(window_kernel, moments()), out_shape=(wh...  13.9 us
    pallas_call x1, Pallas kernels, on_device(): pl.pallas_call(functools.partial(write_kernel, chunk), out_shape=(whole,...  1.72 us

profile of v2, /device:TPU:0, one launch (start us, length us, event | category | flops | bytes accessed | tf_op | source)
XLA Modules:
  0.0 16.3 jit_solution(1751741028960902619)
XLA Ops:
  0.6 13.9 %window.1 = (f32[4,16,24,256]{3,2,1,0:T(8,128)S(1)}, f32[4,16,24,256]{3,2,1,0:T(8,128)S(1)}) custom-call(s32[8]{0:T(128)} %bp_hbm.1, f32[16,24,256]{2,1,0:T(8,128)} %u_hbm.1, f32[16,24,256]{2,1,0:T(8,128)} %d_hbm.1, f32[16,24,256]{2,1,0:T(8,128)} %v_hbm.1, f32[16,24,256]{2,1,0:T(8,128)} %g_hbm.1), custom_call_target="tpu_custom_call" | custom-call | tf_op jit(solution)/shard_map/window/pallas_call | solution.py:314
  14.6 1.7 %write.1 = (f32[4,16,24,256]{3,2,1,0:T(8,128)}, f32[4,16,24,256]{3,2,1,0:T(8,128)}) custom-call(f32[4,16,24,256]{3,2,1,0:T(8,128)S(1)} %get-tuple-element.4.s_ref, f32[4,16,24,256]{3,2,1,0:T(8,128)S(1)} %get-tuple-element.5.f_ref), custom_call_target="tpu_custom_call" | custom-call | tf_op jit(solution)/shard_map/write/pallas_call | solution.py:334

commit v3 on v2

--- a/solution.py
+++ b/solution.py
@@ -10,6 +10,9 @@
 
 M = 8
 step_length = 0.1
+
+U, C, R, Y, FAR = 0, 1, 3, 4, 5
+TRIPS = ((U, U, 1), (C, C, 2), (R, FAR, 1), (R, R, 1), (Y, Y, 1))
 
 
 def legendre_values(order, position):
@@ -105,47 +108,49 @@
 def window_kernel(
     table,
     bp_hbm, u_hbm, d_hbm, v_hbm, g_hbm, s_ref, f_ref,
-    bp, u_ref, d_ref, v_ref, g_ref, r_ref, a_ref, out, got, edge, load_sem, send_sem, recv_sem,
+    bp, u_ref, d_ref, v_ref, g_ref, r_ref, out, got, edge, load_sem, send_sem, recv_sem,
 ):
     me = lax.axis_index("space")
     count = lax.axis_size("space")
-    has_left = me > 0
-    has_right = me < count - 1
     cap = u_ref.shape[0]
     nodes = s_ref.shape[0]
+    quarter = cap // 4
+    pairs = [(bp_hbm, bp)]
+    for i in range(4):
+        part = pl.ds(i * quarter, cap - 3 * quarter if i == 3 else quarter)
+        pairs.append((u_hbm.at[part], u_ref.at[part]))
+    pairs += [(d_hbm, d_ref), (v_hbm, v_ref), (g_hbm, g_ref)]
     loads = [
-        pltpu.make_async_copy(src, dst, load_sem.at[i])
-        for i, (src, dst) in enumerate(
-            [(bp_hbm, bp), (u_hbm, u_ref), (d_hbm, d_ref), (v_hbm, v_ref), (g_hbm, g_ref)]
-        )
+        pltpu.make_async_copy(src, dst, load_sem.at[i]) for i, (src, dst) in enumerate(pairs)
     ]
     for load in loads:
         load.start()
     barrier = pltpu.get_barrier_semaphore()
 
-    @pl.when(has_left)
-    def _():
-        pl.semaphore_signal(
-            barrier, inc=1, device_id={"space": me - 1}, device_id_type=pl.DeviceIdType.MESH
-        )
-
-    @pl.when(has_right)
-    def _():
-        pl.semaphore_signal(
-            barrier, inc=1, device_id={"space": me + 1}, device_id_type=pl.DeviceIdType.MESH
-        )
-
+    def exists(step):
+        return jnp.logical_and(me + step >= 0, me + step < count)
+
+    peers = 0
+    for step in (-1, 1, -2, 2):
+
+        @pl.when(exists(step))
+        def _(step=step):
+            pl.semaphore_signal(
+                barrier, inc=1, device_id={"space": me + step}, device_id_type=pl.DeviceIdType.MESH
+            )
+
+        peers = peers + exists(step).astype(jnp.int32)
     nil = jnp.zeros(u_ref.shape[1:], jnp.float32)
-
-    @pl.when(jnp.logical_not(has_left))
-    def _():
-        for k in range(3):
-            got[k, 0] = nil
-
-    @pl.when(jnp.logical_not(has_right))
-    def _():
-        for k in range(3):
-            got[k, 1] = nil
+    for side, step in ((0, -1), (1, 1)):
+
+        @pl.when(jnp.logical_not(exists(step)))
+        def _(side=side):
+            for k in range(FAR):
+                got[side, k] = nil
+
+        @pl.when(jnp.logical_not(exists(2 * step)))
+        def _(side=side):
+            got[side, FAR] = nil
 
     node = lax.axis_index("node")
     weights = []
@@ -158,54 +163,54 @@
             ]
         weights.append(picked)
 
-    def copy(k, side):
-        return pltpu.make_async_remote_copy(
-            src_ref=out.at[k, side],
-            dst_ref=got.at[k, side],
-            send_sem=send_sem.at[k, side],
-            recv_sem=recv_sem.at[k, side],
-            device_id={"space": me + 1 if side == 0 else me - 1},
+    def copy(side, k):
+        source, target, size = TRIPS[k]
+        distance = 2 if target == FAR else 1
+        step = distance if side == 0 else -distance
+        return step, pltpu.make_async_remote_copy(
+            src_ref=out.at[side, pl.ds(source, size)],
+            dst_ref=got.at[side, pl.ds(target, size)],
+            send_sem=send_sem.at[side, k],
+            recv_sem=recv_sem.at[side, k],
+            device_id={"space": me + step},
             device_id_type=pl.DeviceIdType.MESH,
         )
 
     def send(k):
-        @pl.when(has_right)
-        def _():
-            copy(k, 0).start()
-
-        @pl.when(has_left)
-        def _():
-            copy(k, 1).start()
+        for side in range(2):
+            step, c = copy(side, k)
+
+            @pl.when(exists(step))
+            def _(c=c):
+                c.start()
 
     def receive(k):
-        @pl.when(has_left)
-        def _():
-            copy(k, 0).wait_recv()
-
-        @pl.when(has_right)
-        def _():
-            copy(k, 1).wait_recv()
+        for side in range(2):
+            step, c = copy(side, k)
+
+            @pl.when(exists(-step))
+            def _(c=c):
+                c.wait_recv()
 
     loads[0].wait()
     length = bp[me]
     last = jnp.clip(length - 1, 0, cap - 1)
-
-    def beside(ref, p, k):
-        low = jnp.where(p == 0, got[k, 0], ref[jnp.maximum(p - 1, 0)])
-        high = jnp.where(p == last, got[k, 1], ref[jnp.minimum(p + 1, cap - 1)])
+    single = last == 0
+
+    def inner(ref, p):
+        low = jnp.where(p == 0, 0.0, ref[jnp.maximum(p - 1, 0)])
+        high = jnp.where(p == last, 0.0, ref[jnp.minimum(p + 1, cap - 1)])
         return low, high
 
     def first_rhs(p):
         d, rise, fall, own = factors(d_ref, v_ref, g_ref, p)
-        low, high = beside(u_ref, p, 0)
+        low, high = inner(u_ref, p)
         u = u_ref[p]
         return d * across(u) + rise * high + fall * low + (own - u * u) * u
 
-    def slope(p):
+    def slope(p, r, low, high):
         d, rise, fall, own = factors(d_ref, v_ref, g_ref, p)
-        low, high = beside(r_ref, p, 1)
         u = u_ref[p]
-        r = r_ref[p]
         return d * across(r) + rise * high + fall * low + (own - 3.0 * (u * u)) * r
 
     def states_of(u, r, a):
@@ -214,16 +219,20 @@
         cube = rr * r
         return [u + w[0] * r + w[1] * a + (w[2] * ur + w[3] * cube) for w in weights]
 
-    loads[1].wait()
-    out[0, 0] = u_ref[last]
-    out[0, 1] = u_ref[0]
-    pl.semaphore_wait(barrier, has_left.astype(jnp.int32) + has_right.astype(jnp.int32))
+    for load in loads[1:5]:
+        load.wait()
+    out[0, U] = u_ref[last]
+    out[1, U] = u_ref[0]
+    pl.semaphore_wait(barrier, peers)
     send(0)
-    for load in loads[2:]:
+    for load in loads[5:]:
         load.wait()
-    receive(0)
-    out[1, 0] = first_rhs(last)
-    out[1, 1] = first_rhs(0)
+    _, rise_l, fall_l, _ = factors(d_ref, v_ref, g_ref, last)
+    _, rise_f, fall_f, _ = factors(d_ref, v_ref, g_ref, 0)
+    out[0, C] = rise_l
+    out[0, C + 1] = jnp.where(single, fall_l, 0.0)
+    out[1, C] = fall_f
+    out[1, C + 1] = jnp.where(single, rise_f, 0.0)
     send(1)
 
     def fill_r(p, carry):
@@ -231,13 +240,29 @@
         return carry
 
     lax.fori_loop(0, cap, fill_r, 0)
-    receive(1)
-    out[2, 0] = slope(last)
-    out[2, 1] = slope(0)
+    receive(0)
+    _, rise_l, fall_l, _ = factors(d_ref, v_ref, g_ref, last)
+    _, rise_f, fall_f, _ = factors(d_ref, v_ref, g_ref, 0)
+    r_l = r_ref[last] + rise_l * got[1, U] + jnp.where(single, fall_l * got[0, U], 0.0)
+    r_f = r_ref[0] + fall_f * got[0, U] + jnp.where(single, rise_f * got[1, U], 0.0)
+    out[0, R] = r_l
+    out[1, R] = r_f
     send(2)
+    send(3)
+    r_ref[0] = r_f
+
+    def fix_r(p, carry):
+        r_ref[p] = jnp.where(p == last, out[0, R], r_ref[p])
+        return carry
+
+    lax.fori_loop(0, cap, fix_r, 0)
+    out[0, Y] = slope(last, r_ref[last], *inner(r_ref, last))
+    out[1, Y] = slope(0, r_ref[0], *inner(r_ref, 0))
+    send(4)
 
     def fill_s(p, carry):
-        values = states_of(u_ref[p], r_ref[p], slope(p))
+        r = r_ref[p]
+        values = states_of(u_ref[p], r, slope(p, r, *inner(r_ref, p)))
         live = p < length
         for m in range(nodes):
             s_ref[m, p] = jnp.where(live, values[m], 0.0)
@@ -245,44 +270,79 @@
 
     lax.fori_loop(0, cap, fill_s, 0)
 
+    def final(p, m, low, high):
+        d, rise, fall, own = factors(d_ref, v_ref, g_ref, p)
+        s = s_ref[m, p]
+        f = d * across(s) + rise * high + fall * low + (own - s * s) * s
+        return jnp.where(p < length, f, 0.0)
+
     def fill_f(p, carry):
-        d, rise, fall, own = factors(d_ref, v_ref, g_ref, p)
-        live = p < length
-        down = jnp.maximum(p - 1, 0)
-        up = jnp.minimum(p + 1, cap - 1)
-        fall = jnp.where(p == 0, 0.0, fall)
-        rise = jnp.where(p == cap - 1, 0.0, rise)
         for m in range(nodes):
-            s = s_ref[m, p]
-            f = d * across(s) + rise * s_ref[m, up] + fall * s_ref[m, down] + (own - s * s) * s
-            f_ref[m, p] = jnp.where(live, f, 0.0)
-        return carry
-
-    lax.fori_loop(0, cap, fill_f, 0)
+            low = s_ref[m, jnp.maximum(p - 1, 0)]
+            high = s_ref[m, jnp.minimum(p + 1, cap - 1)]
+            f_ref[m, p] = final(p, m, low, high)
+        return carry
+
+    lax.fori_loop(1, cap - 1, fill_f, 0)
+    receive(3)
+    values = states_of(
+        u_ref[last],
+        r_ref[last],
+        out[0, Y] + rise_l * got[1, R] + jnp.where(single, fall_l * got[0, R], 0.0),
+    )
+    for m in range(nodes):
+        edge[0, m] = values[m]
+    values = states_of(
+        u_ref[0],
+        r_ref[0],
+        out[1, Y] + fall_f * got[0, R] + jnp.where(single, rise_f * got[1, R], 0.0),
+    )
+    for m in range(nodes):
+        s_ref[m, 0] = values[m]
+
+    def fix_s(p, carry):
+        for m in range(nodes):
+            s_ref[m, p] = jnp.where(p == last, edge[0, m], s_ref[m, p])
+        return carry
+
+    lax.fori_loop(0, cap, fix_s, 0)
+    receive(1)
     receive(2)
-    _, _, fall, _ = factors(d_ref, v_ref, g_ref, 0)
-    values = states_of(got[0, 0], got[1, 0], got[2, 0])
+    receive(4)
+    for side, r in ((0, r_ref[0]), (1, r_ref[last])):
+        a = got[side, Y] + got[side, C] * r + got[side, C + 1] * got[side, FAR]
+        values = states_of(got[side, U], got[side, R], a)
+        for m in range(nodes):
+            edge[1 + side, m] = values[m]
+
+    def rim(p, m):
+        low = jnp.where(p == 0, edge[1, m], s_ref[m, jnp.maximum(p - 1, 0)])
+        high = jnp.where(p == last, edge[2, m], s_ref[m, jnp.minimum(p + 1, cap - 1)])
+        return final(p, m, low, high)
+
+    near = jnp.maximum(last - 1, 0)
     for m in range(nodes):
-        f_ref[m, 0] += fall * values[m]
-    _, rise, _, _ = factors(d_ref, v_ref, g_ref, last)
-    values = states_of(got[0, 1], got[1, 1], got[2, 1])
+        f_ref[m, 0] = rim(0, m)
+        f_ref[m, 1] = rim(1, m)
+        edge[3, m] = rim(near, m)
+        edge[4, m] = rim(last, m)
+
+    def fix_f(p, carry):
+        for m in range(nodes):
+            f = jnp.where(p == near, edge[3, m], f_ref[m, p])
+            f_ref[m, p] = jnp.where(p == last, edge[4, m], f)
+        return carry
+
+    lax.fori_loop(0, cap - 1, fix_f, 0)
     for m in range(nodes):
-        edge[m] = rise * values[m]
-
-    def fix(p, carry):
-        for m in range(nodes):
-            f_ref[m, p] += jnp.where(p == last, edge[m], 0.0)
-        return carry
-
-    lax.fori_loop(0, cap, fix, 0)
-    for k in range(3):
-        @pl.when(has_right)
-        def _(k=k):
-            copy(k, 0).wait_send()
-
-        @pl.when(has_left)
-        def _(k=k):
-            copy(k, 1).wait_send()
+        f_ref[m, cap - 1] = jnp.where(last == cap - 1, edge[4, m], 0.0)
+    for k in range(len(TRIPS)):
+        for side in range(2):
+            step, c = copy(side, k)
+
+            @pl.when(exists(step))
+            def _(c=c):
+                c.wait_send()
 
 
 def write_kernel(chunk, s_ref, f_ref, s_hbm, f_hbm, sem):
@@ -317,14 +377,14 @@
         in_specs=[hbm] * 5,
         out_specs=(vmem, vmem),
         scratch_shapes=[pltpu.SMEM(block_planes.shape, jnp.int32)]
-        + [pltpu.VMEM(shape, jnp.float32)] * 6
+        + [pltpu.VMEM(shape, jnp.float32)] * 5
         + [
-            pltpu.VMEM((3, 2) + plane, jnp.float32),
-            pltpu.VMEM((3, 2) + plane, jnp.float32),
-            pltpu.VMEM((nodes,) + plane, jnp.float32),
-            pltpu.SemaphoreType.DMA((5,)),
-            pltpu.SemaphoreType.DMA((3, 2)),
-            pltpu.SemaphoreType.DMA((3, 2)),
+            pltpu.VMEM((2, FAR) + plane, jnp.float32),
+            pltpu.VMEM((2, FAR + 1) + plane, jnp.float32),
+            pltpu.VMEM((5, nodes) + plane, jnp.float32),
+            pltpu.SemaphoreType.DMA((8,)),
+            pltpu.SemaphoreType.DMA((2, len(TRIPS))),
+            pltpu.SemaphoreType.DMA((2, len(TRIPS))),
         ],
         compiler_params=pltpu.CompilerParams(
             collective_id=0, has_side_effects=True, vmem_limit_bytes=24 << 20

time: 16.5 us -> 14.2 us (0.86)
  Pallas kernels: 15.7 us -> 13.4 us
    pallas_call x1, Pallas kernels: 13.9 us -> 11.7 us  [on_device(): pl.pallas_call(functools.partial(window_kernel, moments()), out_shape=(wh...]
where the time goes in v3:
time: 14.2 us; the launch traced here: 14.1 us
  Pallas kernels  13.4 us (94%)
  between operations  0.64 us (5%)
    pallas_call x1, Pallas kernels, on_device(): pl.pallas_call(functools.partial(window_kernel, moments()), out_shape=(wh...  11.7 us
    pallas_call x1, Pallas kernels, on_device(): pl.pallas_call(functools.partial(write_kernel, chunk), out_shape=(whole,...  1.72 us

profile of v3, /device:TPU:0, one launch (start us, length us, event | category | flops | bytes accessed | tf_op | source)
XLA Modules:
  0.0 14.1 jit_solution(16002544077295822075)
XLA Ops:
  0.6 11.7 %window.1 = (f32[4,16,24,256]{3,2,1,0:T(8,128)S(1)}, f32[4,16,24,256]{3,2,1,0:T(8,128)S(1)}) custom-call(s32[8]{0:T(128)} %bp_hbm.1, f32[16,24,256]{2,1,0:T(8,128)} %u_hbm.1, f32[16,24,256]{2,1,0:T(8,128)} %d_hbm.1, f32[16,24,256]{2,1,0:T(8,128)} %v_hbm.1, f32[16,24,256]{2,1,0:T(8,128)} %g_hbm.1), custom_call_target="tpu_custom_call" | custom-call | tf_op jit(solution)/shard_map/window/pallas_call | solution.py:374
  12.3 1.7 %write.1 = (f32[4,16,24,256]{3,2,1,0:T(8,128)}, f32[4,16,24,256]{3,2,1,0:T(8,128)}) custom-call(f32[4,16,24,256]{3,2,1,0:T(8,128)S(1)} %get-tuple-element.4.s_ref, f32[4,16,24,256]{3,2,1,0:T(8,128)S(1)} %get-tuple-element.5.f_ref), custom_call_target="tpu_custom_call" | custom-call | tf_op jit(solution)/shard_map/write/pallas_call | solution.py:394

commit v4 on v3

--- a/solution.py
+++ b/solution.py
@@ -363,7 +363,7 @@
     shape = initial.shape
     plane = shape[1:]
     nodes = M // lax.axis_size("node")
-    chunk = 4
+    chunk = 2
     operands = [
         pltpu.with_memory_space_constraint(x, pltpu.HBM)
         for x in (block_planes, initial, diffusivity, velocity, growth_rate)

time: 14.2 us -> 14.3 us (level)
  no operation moved by 1% of the time
where the time goes in v4:
time: 14.3 us; the launch traced here: 14.1 us
  Pallas kernels  13.5 us (94%)
  between operations  0.64 us (4%)
    pallas_call x1, Pallas kernels, on_device(): pl.pallas_call(functools.partial(window_kernel, moments()), out_shape=(wh...  11.7 us
    pallas_call x1, Pallas kernels, on_device(): pl.pallas_call(functools.partial(write_kernel, chunk), out_shape=(whole,...  1.79 us

profile of v4, /device:TPU:0, one launch (start us, length us, event | category | flops | bytes accessed | tf_op | source)
XLA Modules:
  0.0 14.1 jit_solution(12984666166900289259)
XLA Ops:
  0.6 11.7 %window.1 = (f32[4,16,24,256]{3,2,1,0:T(8,128)S(1)}, f32[4,16,24,256]{3,2,1,0:T(8,128)S(1)}) custom-call(s32[8]{0:T(128)} %bp_hbm.1, f32[16,24,256]{2,1,0:T(8,128)} %u_hbm.1, f32[16,24,256]{2,1,0:T(8,128)} %d_hbm.1, f32[16,24,256]{2,1,0:T(8,128)} %v_hbm.1, f32[16,24,256]{2,1,0:T(8,128)} %g_hbm.1), custom_call_target="tpu_custom_call" | custom-call | tf_op jit(solution)/shard_map/window/pallas_call | solution.py:374
  12.3 1.8 %write.1 = (f32[4,16,24,256]{3,2,1,0:T(8,128)}, f32[4,16,24,256]{3,2,1,0:T(8,128)}) custom-call(f32[4,16,24,256]{3,2,1,0:T(8,128)S(1)} %get-tuple-element.4.s_ref, f32[4,16,24,256]{3,2,1,0:T(8,128)S(1)} %get-tuple-element.5.f_ref), custom_call_target="tpu_custom_call" | custom-call | tf_op jit(solution)/shard_map/write/pallas_call | solution.py:394

commit v5 on v3

--- a/solution.py
+++ b/solution.py
@@ -251,14 +251,16 @@
     send(3)
     r_ref[0] = r_f
 
+    out[0, Y] = slope(last, out[0, R], *inner(r_ref, last))
+    low, high = inner(r_ref, 0)
+    out[1, Y] = slope(0, r_ref[0], low, jnp.where(last == 1, out[0, R], high))
+    send(4)
+
     def fix_r(p, carry):
         r_ref[p] = jnp.where(p == last, out[0, R], r_ref[p])
         return carry
 
     lax.fori_loop(0, cap, fix_r, 0)
-    out[0, Y] = slope(last, r_ref[last], *inner(r_ref, last))
-    out[1, Y] = slope(0, r_ref[0], *inner(r_ref, 0))
-    send(4)
 
     def fill_s(p, carry):
         r = r_ref[p]

time: 14.2 us -> 14.2 us (level)
  no operation moved by 1% of the time
where the time goes in v5:
time: 14.2 us; the launch traced here: 14.1 us
  Pallas kernels  13.4 us (94%)
  between operations  0.64 us (5%)
    pallas_call x1, Pallas kernels, on_device(): pl.pallas_call(functools.partial(window_kernel, moments()), out_shape=(wh...  11.7 us
    pallas_call x1, Pallas kernels, on_device(): pl.pallas_call(functools.partial(write_kernel, chunk), out_shape=(whole,...  1.72 us

profile of v5, /device:TPU:0, one launch (start us, length us, event | category | flops | bytes accessed | tf_op | source)
XLA Modules:
  0.0 14.1 jit_solution(10652303147471230625)
XLA Ops:
  0.6 11.7 %window.1 = (f32[4,16,24,256]{3,2,1,0:T(8,128)S(1)}, f32[4,16,24,256]{3,2,1,0:T(8,128)S(1)}) custom-call(s32[8]{0:T(128)} %bp_hbm.1, f32[16,24,256]{2,1,0:T(8,128)} %u_hbm.1, f32[16,24,256]{2,1,0:T(8,128)} %d_hbm.1, f32[16,24,256]{2,1,0:T(8,128)} %v_hbm.1, f32[16,24,256]{2,1,0:T(8,128)} %g_hbm.1), custom_call_target="tpu_custom_call" | custom-call | tf_op jit(solution)/shard_map/window/pallas_call | solution.py:376
  12.3 1.7 %write.1 = (f32[4,16,24,256]{3,2,1,0:T(8,128)}, f32[4,16,24,256]{3,2,1,0:T(8,128)}) custom-call(f32[4,16,24,256]{3,2,1,0:T(8,128)S(1)} %get-tuple-element.4.s_ref, f32[4,16,24,256]{3,2,1,0:T(8,128)S(1)} %get-tuple-element.5.f_ref), custom_call_target="tpu_custom_call" | custom-call | tf_op jit(solution)/shard_map/write/pallas_call | solution.py:396
